TPU v7x, 32 devices: a whole 2x2x4 slice. The times are simulated.
32 devices in a mesh: space: 8 (over y, x, core), chan: 4 (over z).
Axes of the slice: x: 2, y: 2, z: 4, core: 2. Of those that a mesh axis runs over, the one named last changes fastest.
Arguments:
- images: bfloat16 [768, 64, 256], P('chan', 'space'), may hold values from -6 to 6
- weight: bfloat16 [3, 3, 768, 768], P(None, None, 'chan'), may hold values from -0.078125 to 0.078125
- cotangent: bfloat16 [768, 64, 256], P('chan', 'space'), may hold values from -6 to 6
Outputs:
- activated: bfloat16 [768, 64, 256], P('chan', 'space')
- input_grad: bfloat16 [768, 64, 256], P('chan', 'space')
- weight_grad: float32 [3, 3, 768, 768], P(None, None, 'chan')
All inputs are finite; a program needn't handle non-finite values.
Results may differ from a plain program's by a relative error of at most 0.005.
Values may be sent and summed in bfloat16 or wider, within the bound.
A program may use at most 128 MiB of HBM per device.

v0:
```python
import jax
import jax.numpy as jnp
from jax import lax
from jax.sharding import PartitionSpec as P


def with_halo(array, sides, width):
    for axis, dim in sides:
        peers, length = (lax.axis_size(axis), array.shape[dim])
        up = [(i, (i + 1) % peers) for i in range(peers - 1)]
        down = [(j, i) for i, j in up]
        last = lax.slice_in_dim(array, length - width, length, axis=dim)
        leading = lax.slice_in_dim(array, 0, width, axis=dim)
        before = lax.ppermute(last, axis, up)
        after = lax.ppermute(leading, axis, down)
        array = jnp.concatenate([before, array, after], axis=dim)
    return array


def widen(block):
    return jnp.pad(block, ((0, 0), (0, 0), (1, 1)))


def forward_add(total, piece, weight):
    rows = total.shape[1]
    width = total.shape[2]
    wide = widen(piece)
    for row_tap in range(3):
        for col_tap in range(3):
            total = total + jnp.einsum(
                "oi,ihw->ohw",
                weight[row_tap, col_tap],
                wide[:, row_tap : row_tap + rows, col_tap : col_tap + width],
                preferred_element_type=jnp.float32,
            )
    return total


def wgrad_add(piece, gradient):
    rows = gradient.shape[1]
    width = gradient.shape[2]
    wide = widen(piece)
    taps = []
    for row_tap in range(3):
        line = []
        for col_tap in range(3):
            line.append(
                jnp.einsum(
                    "ihw,ohw->oi",
                    wide[:, row_tap : row_tap + rows, col_tap : col_tap + width],
                    gradient,
                    preferred_element_type=jnp.float32,
                )
            )
        taps.append(jnp.stack(line))
    terms = jnp.stack(taps)
    return terms


def transpose_taps(kernel, wide, rows, width):
    total = None
    for row_tap in range(3):
        for col_tap in range(3):
            term = jnp.einsum(
                "oi,ohw->ihw",
                kernel[row_tap, col_tap],
                wide[:, 2 - row_tap : 2 - row_tap + rows, 2 - col_tap : 2 - col_tap + width],
                preferred_element_type=jnp.float32,
            )
            total = term if total is None else total + term
    return total


def on_device(images, weight, cotangent):
    block = images.shape[0]
    rows = images.shape[1]
    width = images.shape[2]
    framed = with_halo(images, (("space", 1),), 1)
    empty = jnp.zeros((block, rows, width), jnp.float32)
    pre = forward_add(empty, lax.all_gather(framed, "chan", axis=0, tiled=True), weight)
    sigma = jax.nn.sigmoid(pre)
    activated = (pre * sigma).astype(jnp.bfloat16)
    pre_grad = (cotangent.astype(jnp.float32) * sigma * (1.0 + pre * (1.0 - sigma))).astype(
        jnp.bfloat16
    )
    local_wgrad = wgrad_add(lax.all_gather(framed, "chan", axis=0, tiled=True), pre_grad)
    grad_framed = with_halo(pre_grad, (("space", 1),), 1)
    grad_wide = widen(grad_framed)
    input_sum = lax.psum_scatter(
        transpose_taps(weight, grad_wide, rows, width), "chan", scatter_dimension=0, tiled=True
    )
    weight_grad = lax.psum(local_wgrad, "space")
    return (activated, input_sum.astype(jnp.bfloat16), weight_grad)


def solution(mesh):
    return jax.shard_map(
        on_device,
        mesh=mesh,
        in_specs=(P("chan", "space", None), P(None, None, "chan", None), P("chan", "space", None)),
        out_specs=(P("chan", "space", None), P("chan", "space", None), P(None, None, "chan", None)),
        check_vma=False,
    )
```

profile of v0, /device:TPU:0, one launch (start us, length us, event | category | flops | bytes accessed | tf_op | source)
XLA Modules:
  0.0 394.3 jit_solution(2143091007980894308)
XLA Ops:
  7.2 1.4 copy.12
  8.7 1.3 collective-permute-start.1
  10.0 3.0 collective-permute-start
  15.1 82.7 %all-gather.2.cloned.1.call-done = bf16[768,10,256]{2,0,1:T(8,128)(2,1)} async-done(((bf16[192,10,256]{2,0,1:T(8,128)(2,1)}), bf16[768,10,256]{2,0,1:T(8,128)(2,1)}) %all-gather.2.cloned.1.call-update) | async-done | bytes 3932176 | tf_op jit(solution)/shard_map/all_gather | solution.py:80
  97.8 2.8 fusion.3
  109.4 2.3 fusion.34
  111.7 1.8 collective-permute-start.2
  113.5 1.5 collective-permute-start.3
  115.0 3.6 fusion.84
  119.5 4.1 %fusion.64 = f32[8,256,768]{2,1,0:T(8,128)} fusion(bf16[192,10,258]{2,0,1:T(8,128)(2,1)S(1)} %fusion.36, bf16[3,3,192,768]{3,2,1,0:T(8,128)(2,1)S(1)} %copy-done.3), kind=kOutput, calls=%fused_computation.74 | convolution fusion | flops 603979776 | bytes 7372800 | tf_op jit(solution)/shard_map/oi,ohw->ihw/dot_general | solution.py:64
  123.5 3.7 fusion.66
  127.2 4.0 %fusion.68 = f32[8,256,768]{2,1,0:T(8,128)} fusion(bf16[192,10,258]{2,0,1:T(8,128)(2,1)S(1)} %fusion.36, bf16[3,3,192,768]{3,2,1,0:T(8,128)(2,1)S(1)} %copy-done.3), kind=kOutput, calls=%fused_computation.78 | convolution fusion | flops 603979776 | bytes 7372800 | tf_op jit(solution)/shard_map/oi,ohw->ihw/dot_general | solution.py:64
  131.2 3.7 fusion.70
  134.9 4.1 %fusion.72 = f32[8,256,768]{2,1,0:T(8,128)} fusion(bf16[192,10,258]{2,0,1:T(8,128)(2,1)S(1)} %fusion.36, bf16[3,3,192,768]{3,2,1,0:T(8,128)(2,1)S(1)} %copy-done.3), kind=kOutput, calls=%fused_computation.82 | convolution fusion | flops 603979776 | bytes 7372800 | tf_op jit(solution)/shard_map/oi,ohw->ihw/dot_general | solution.py:64
  139.0 3.6 fusion.56
  142.7 3.7 fusion.52
  146.3 19.7 %add_bitcast_fusion = f32[768,8,256]{0,2,1:T(8,128)} fusion(f32[8,256,768]{2,1,0:T(8,128)} %fusion.56, f32[8,256,768]{2,1,0:T(8,128)} %fusion.64, f32[8,256,768]{2,1,0:T(8,128)} %fusion.66, f32[8,256,768]{2,1,0:T(8,128)} %fusion.84, f32[8,256,768]{2,1,0:T(8,128)} %fusion.68, f32[8,256,768]{2,1,0:T(8,128)} %fusion.70, f32[8,256,768]{2,1,0:T(8,128)} %fusion.72, ...), kind=kOutput, calls=%fused_computation.6 | convolution fusion | flops 616562688 | bytes 57704448 | tf_op jit(solution)/shard_map/oi,ohw->ihw/dot_general | solution.py:64
  166.0 6.7 %copy.16 = f32[768,8,256]{2,1,0:T(8,128)} copy(f32[768,8,256]{0,2,1:T(8,128)} %add_bitcast_fusion) | data formatting | bytes 12582912 | tf_op jit(solution)/shard_map/add | solution.py:70
  173.0 3.4 fusion.37
  176.4 1.4 fusion.38
  179.1 1.4 fusion.41
  180.5 1.4 fusion.42
  181.9 1.4 fusion.39
  183.3 1.4 fusion.40
  184.7 1.2 fusion.43
  185.8 1.2 fusion.46
  187.2 2.7 pad_maximum_fusion
  190.0 1.3 copy.17
  191.3 93.4 %reduce-scatter.2.cloned.1.call-done = f32[192,8,256]{2,1,0:T(8,128)} async-done(((f32[768,8,256]{2,1,0:T(8,128)}), f32[192,8,256]{2,1,0:T(8,128)}) %reduce-scatter.2.cloned.1.call-update) | async-done | bytes 1572880 | tf_op jit(solution)/shard_map/reduce_scatter | solution.py:89
  284.7 2.4 convert_element_type.20
  287.0 95.6 %all-reduce.4.cloned.1.call-done = f32[3,3,192,768]{3,2,1,0:T(8,128)} async-done(((f32[3,3,192,768]{3,2,1,0:T(8,128)}), f32[3,3,192,768]{3,2,1,0:T(8,128)}) %all-reduce.4.cloned.1.call-update) | async-done | bytes 5308432 | tf_op jit(solution)/shard_map/psum | solution.py:92
  382.6 5.2 %copy.20 = f32[3,3,192,768]{3,2,1,0:T(8,128)} copy(f32[3,3,192,768]{3,2,1,0:T(8,128)} %all-reduce.4.cloned.1.call-done) | data formatting | bytes 10616832
  (34 shorter events, 13.5 us)
Async XLA Ops:
  7.2 90.6 %copy-start.2 = (bf16[3,3,192,768]{3,2,1,0:T(8,128)(2,1)S(1)}, bf16[3,3,192,768]{3,2,1,0:T(8,128)(2,1)}, u32[]{:S(2)}) copy-start(bf16[3,3,192,768]{3,2,1,0:T(8,128)(2,1)} %param.4) | copy-start | bytes 7962628
  7.2 90.6 %all-gather.2.cloned.1.call-start = ((), (), s32[]{:S(2)}) async-start(), calls=%async_computation.1 | async-start | bytes 4915200 | tf_op jit(solution)/shard_map/all_gather | solution.py:80
  8.7 4.3 %collective-permute-start.1 = (bf16[192,1,256]{2,0,1:T(8,128)(2,1)S(1)}, bf16[192,1,256]{2,0,1:T(8,128)(2,1)S(1)}, u32[]{:S(2)}, u32[]{:S(2)}) collective-permute-start(bf16[192,1,256]{2,0,1:T(8,128)(2,1)S(1)} %get-tuple-element.14), channel_id=1, source_target_pairs={{4,0},{8,4},{12,8},{16,12},{20,16},{24,20},{28,24},{5,1},{9,5},{13... | collective-permute-start | bytes 294920 | tf_op jit(solution)/shard_map/ppermute | solution.py:15
  10.0 4.0 %collective-permute-start = (bf16[192,1,256]{2,0,1:T(8,128)(2,1)S(1)}, bf16[192,1,256]{2,0,1:T(8,128)(2,1)S(1)}, u32[]{:S(2)}, u32[]{:S(2)}) collective-permute-start(bf16[192,1,256]{2,0,1:T(8,128)(2,1)S(1)} %get-tuple-element.13), channel_id=1, source_target_pairs={{0,4},{4,8},{8,12},{12,16},{16,20},{20,24},{24,28},{1,5},{5,9},{9,... | collective-permute-start | bytes 294920 | tf_op jit(solution)/shard_map/ppermute | solution.py:14
  15.0 269.6 %reduce-scatter.2.cloned.1.call-start = ((), (), s32[]{:S(2)}) async-start(), calls=%async_computation.2 | async-start | bytes 7864320 | tf_op jit(solution)/shard_map/reduce_scatter | solution.py:89
  97.8 3.1 copy-start
  107.4 1.8 copy-start.3
  107.4 1.9 copy-start.4
  111.7 6.9 %collective-permute-start.2 = (bf16[192,1,256]{2,0,1:T(8,128)(2,1)S(1)}, bf16[192,1,256]{2,0,1:T(8,128)(2,1)S(1)}, u32[]{:S(2)}, u32[]{:S(2)}) collective-permute-start(bf16[192,1,256]{2,0,1:T(8,128)(2,1)S(1)} %get-tuple-element.12), channel_id=1, source_target_pairs={{0,4},{4,8},{8,12},{12,16},{16,20},{20,24},{24,28},{1,5},{5,9},{9,... | collective-permute-start | bytes 294920 | tf_op jit(solution)/shard_map/ppermute | solution.py:14
  113.5 5.1 %collective-permute-start.3 = (bf16[192,1,256]{2,0,1:T(8,128)(2,1)S(1)}, bf16[192,1,256]{2,0,1:T(8,128)(2,1)S(1)}, u32[]{:S(2)}, u32[]{:S(2)}) collective-permute-start(bf16[192,1,256]{2,0,1:T(8,128)(2,1)S(1)} %get-tuple-element.11), channel_id=1, source_target_pairs={{4,0},{8,4},{12,8},{16,12},{20,16},{24,20},{28,24},{5,1},{9,5},{13... | collective-permute-start | bytes 294920 | tf_op jit(solution)/shard_map/ppermute | solution.py:15
  172.7 209.9 %all-reduce.4.cloned.1.call-start = ((), (), s32[]{:S(2)}) async-start(), calls=%async_computation.3 | async-start | bytes 10616832 | tf_op jit(solution)/shard_map/psum | solution.py:92
  172.9 3.4 copy-start.1
Sparse Core Ops, SparseCore 0:
  15.2 82.5 all-gather.1
  172.8 111.8 reduce-scatter.1
  288.6 93.9 all-reduce.3
where the time goes:
time: 395 us; the launch traced here: 394 us
  waiting for transfers between devices  273 us (69%)
  matrix products  76.5 us (19%)
  local copies, waits for them, and re-layouts  16 us (4%)
  between operations  14 us (4%)
  starting transfers between devices  7.9 us (2%)
  other arithmetic  7.35 us (2%)
    psum x1, waiting for transfers between devices, on_device(): weight_grad = lax.psum(local_wgrad, 'space')  95.6 us
    reduce_scatter x1, waiting for transfers between devices, on_device(): lax.psum_scatter(transpose_taps(weight, grad_wide, rows, width), 'chan',...  93.4 us
    all_gather x1, waiting for transfers between devices, on_device(): lax.all_gather(framed, 'chan', axis=0, tiled=True)  82.7 us
    dot_general x9, matrix products, transpose_taps(): jnp.einsum('oi,ohw->ihw', kernel[row_tap, col_tap], wide[:, 2 - row_tap:2...  50.2 us
    dot_general x9, matrix products, wgrad_add(): jnp.einsum('ihw,ohw->oi', wide[:, row_tap:row_tap + rows, col_tap:col_tap...  13.9 us
    dot_general x9, matrix products, forward_add(): jnp.einsum('oi,ihw->ohw', weight[row_tap, col_tap], wide[:, row_tap:row_t...  12.5 us
    unnamed x13, local copies, waits for them, and re-layouts  9.35 us
  transfers between devices with their start and end apart: 7, of which 4 were waited for; matrix products, arithmetic and copies ran while one was open for 6% of the time, Pallas kernels for 0%

commit v1 on v0

--- a/solution.py
+++ b/solution.py
@@ -75,22 +75,22 @@
     block = images.shape[0]
     rows = images.shape[1]
     width = images.shape[2]
-    framed = with_halo(images, (("space", 1),), 1)
+    gathered = lax.all_gather(images, "chan", axis=0, tiled=True)
+    framed = with_halo(gathered, (("space", 1),), 1)
     empty = jnp.zeros((block, rows, width), jnp.float32)
-    pre = forward_add(empty, lax.all_gather(framed, "chan", axis=0, tiled=True), weight)
+    pre = forward_add(empty, framed, weight)
     sigma = jax.nn.sigmoid(pre)
     activated = (pre * sigma).astype(jnp.bfloat16)
     pre_grad = (cotangent.astype(jnp.float32) * sigma * (1.0 + pre * (1.0 - sigma))).astype(
         jnp.bfloat16
     )
-    local_wgrad = wgrad_add(lax.all_gather(framed, "chan", axis=0, tiled=True), pre_grad)
     grad_framed = with_halo(pre_grad, (("space", 1),), 1)
     grad_wide = widen(grad_framed)
-    input_sum = lax.psum_scatter(
-        transpose_taps(weight, grad_wide, rows, width), "chan", scatter_dimension=0, tiled=True
-    )
-    weight_grad = lax.psum(local_wgrad, "space")
-    return (activated, input_sum.astype(jnp.bfloat16), weight_grad)
+    partial = transpose_taps(weight, grad_wide, rows, width).astype(jnp.bfloat16)
+    input_grad = lax.psum_scatter(partial, "chan", scatter_dimension=0, tiled=True)
+    local_wgrad = wgrad_add(framed, pre_grad).astype(jnp.bfloat16)
+    weight_grad = lax.psum(local_wgrad, "space").astype(jnp.float32)
+    return (activated, input_grad, weight_grad)
 
 
 def solution(mesh):

time: 395 us -> 263 us (0.67)
  waiting for transfers between devices: 273 us -> 136 us
  starting transfers between devices: 7.9 us -> 14.6 us
  other arithmetic: 7.35 us -> 11.5 us
    psum x1, waiting for transfers between devices: 95.6 us -> 9.79 us  [on_device(): weight_grad = lax.psum(local_wgrad, 'space').astype(jnp.float32)]
    reduce_scatter x1, waiting for transfers between devices: 93.4 us -> 58.4 us  [on_device(): lax.psum_scatter(partial, 'chan', scatter_dimension=0, tiled=True)]
    all_gather x1, waiting for transfers between devices: 82.7 us -> 66.7 us  [on_device(): gathered = lax.all_gather(images, 'chan', axis=0, tiled=True)]
    ppermute x2, starting transfers between devices: 4.79 us -> 11.7 us  [with_halo(): before = lax.ppermute(last, axis, up)]
    add x1 -> x0, local copies, waits for them, and re-layouts: 6.65 us -> none  [transpose_taps(): total = term if total is None else total + term]
    convert_element_type x0 -> x1, local copies, waits for them, and re-layouts: none -> 5.11 us  [on_device(): transpose_taps(weight, grad_wide, rows, width).astype(jnp.bfloat16)]
    unnamed x13 -> x12, local copies, waits for them, and re-layouts: 9.35 us -> 5.11 us
  transfers between devices with their start and end apart: 7 -> 7, of which waited for: 4 -> 4; matrix products, arithmetic and copies ran while one was open for 6% -> 26% of each run, Pallas kernels for 0% -> 0%
where the time goes in v1:
time: 263 us
  waiting for transfers between devices  136 us (52%)
  matrix products  74.3 us (28%)
  starting transfers between devices  14.6 us (6%)
  between operations  14 us (5%)
  local copies, waits for them, and re-layouts  12.2 us (5%)
  other arithmetic  11.5 us (4%)
    all_gather x1, waiting for transfers between devices, on_device(): gathered = lax.all_gather(images, 'chan', axis=0, tiled=True)  66.7 us
    reduce_scatter x1, waiting for transfers between devices, on_device(): lax.psum_scatter(partial, 'chan', scatter_dimension=0, tiled=True)  58.4 us
    dot_general x9, matrix products, transpose_taps(): jnp.einsum('oi,ohw->ihw', kernel[row_tap, col_tap], wide[:, 2 - row_tap:2...  50.6 us
    dot_general x9, matrix products, forward_add(): jnp.einsum('oi,ihw->ohw', weight[row_tap, col_tap], wide[:, row_tap:row_t...  12.2 us
    ppermute x2, starting transfers between devices, with_halo(): before = lax.ppermute(last, axis, up)  11.7 us
    dot_general x9, matrix products, wgrad_add(): jnp.einsum('ihw,ohw->oi', wide[:, row_tap:row_tap + rows, col_tap:col_tap...  11.5 us
    psum x1, waiting for transfers between devices, on_device(): weight_grad = lax.psum(local_wgrad, 'space').astype(jnp.float32)  9.79 us
  transfers between devices with their start and end apart: 7, of which 4 were waited for; matrix products, arithmetic and copies ran while one was open for 26% of the time, Pallas kernels for 0%

profile of v1, /device:TPU:0, one launch (start us, length us, event | category | flops | bytes accessed | tf_op | source)
XLA Modules:
  0.0 262.5 jit_solution(5596210124037628629)
XLA Ops:
  7.2 2.3 copy.10
  9.6 66.7 %all-gather.2.cloned.1.call-done = bf16[768,8,256]{2,0,1:T(8,128)(2,1)} async-done(((bf16[192,8,256]{2,0,1:T(8,128)(2,1)}), bf16[768,8,256]{2,0,1:T(8,128)(2,1)}) %all-gather.2.cloned.1.call-update) | async-done | bytes 3145744 | tf_op jit(solution)/shard_map/all_gather | solution.py:78
  76.4 1.3 fusion.171
  77.7 1.8 collective-permute-start
  79.4 1.3 collective-permute-start.1
  80.8 2.7 %fusion.137 = f32[192,8,256]{2,0,1:T(8,128)S(1)} fusion(bf16[768,8,256]{2,0,1:T(8,128)(2,1)} %all-gather.2.cloned.1.call-done, bf16[3,3,192,768]{3,2,1,0:T(8,128)(2,1)S(1)} %copy-done.1), kind=kOutput, calls=%fused_computation.117 | convolution fusion | flops 603979776 | bytes 5013504 | tf_op jit(solution)/shard_map/oi,ihw->ohw/dot_general | solution.py:30
  84.3 4.0 %fusion.5 = bf16[768,10,258]{2,0,1:T(8,128)(2,1)S(1)} fusion(bf16[768,1,256]{2,0,1:T(8,128)(2,1)S(1)} %collective-permute-done.1, bf16[768,8,256]{2,0,1:T(8,128)(2,1)S(1)} %copy-done, bf16[768,1,256]{2,0,1:T(8,128)(2,1)S(1)} %collective-permute-done), kind=kLoop, calls=%fused_computation.8 | loop fusion | flops 23777280 | bytes 7895040 | tf_op jit(solution)/shard_map/concatenate | solution.py:16
  89.1 1.2 fusion.18
  91.1 1.2 fusion.26
  95.1 3.1 %multiply_convert_fusion = (bf16[192,8,256]{2,0,1:T(8,128)(2,1)S(1)}, bf16[192,8,256]{2,0,1:T(8,128)(2,1)}) fusion(bf16[192,8,256]{2,1,0:T(8,128)(2,1)S(1)} %copy-done.4, bf16[768,10,258]{2,0,1:T(8,128)(2,1)S(1)} %fusion.5, bf16[3,3,192,768]{3,2,1,0:T(8,128)(2,1)S(1)} %copy-done.1, f32[8,256,192]{1,2,0:T(8,128)S(1)} %fusion.34, ...), kind=kOutput, calls=%fused_computation.52 | convolution fusion | flops 611844096 | bytes 18382848 | tf_op jit(solution)/shard_map/oi,ihw->ohw/dot_general | solution.py:30
  100.1 1.5 fusion.96
  102.7 1.5 fusion.90
  104.2 1.2 fusion.87
  105.4 1.5 fusion.102
  106.9 3.7 %fusion.135 = f32[8,256,768]{2,1,0:T(8,128)} fusion(bf16[192,8,256]{2,0,1:T(8,128)(2,1)S(1)} %get-tuple-element.11, bf16[3,3,192,768]{3,2,1,0:T(8,128)(2,1)S(1)} %copy-done.1), kind=kOutput, calls=%fused_computation.115 | convolution fusion | flops 603979776 | bytes 7372800 | tf_op jit(solution)/shard_map/oi,ohw->ihw/dot_general | solution.py:64
  110.6 1.3 collective-permute-start.3
  111.9 10.0 %collective-permute-start.2 = (bf16[192,1,256]{2,0,1:T(8,128)(2,1)S(1)}, bf16[192,1,256]{2,0,1:T(8,128)(2,1)S(1)}, u32[]{:S(2)}, u32[]{:S(2)}) collective-permute-start(bf16[192,1,256]{2,0,1:T(8,128)(2,1)S(1)} %get-tuple-element.14), channel_id=1, source_target_pairs={{0,4},{4,8},{8,12},{12,16},{16,20},{20,24},{24,28},{1,5},{5,9},{9,... | collective-permute-start | bytes 294920 | tf_op jit(solution)/shard_map/ppermute | solution.py:14
  121.8 1.2 fusion.84
  125.7 1.8 pad_maximum_fusion.2
  128.7 5.1 %fusion.117 = f32[8,256,768]{2,1,0:T(8,128)} fusion(bf16[192,10,258]{2,0,1:T(8,128)(2,1)S(1)} %fusion.42, bf16[3,3,192,768]{3,2,1,0:T(8,128)(2,1)} %param.4), kind=kOutput, calls=%fused_computation.97 | convolution fusion | flops 603979776 | bytes 7372800 | tf_op jit(solution)/shard_map/oi,ohw->ihw/dot_general | solution.py:64
  133.8 3.6 %fusion.119 = f32[8,256,768]{2,1,0:T(8,128)} fusion(bf16[192,10,258]{2,0,1:T(8,128)(2,1)S(1)} %fusion.42, bf16[3,3,192,768]{3,2,1,0:T(8,128)(2,1)S(1)} %copy-done.2), kind=kOutput, calls=%fused_computation.99 | convolution fusion | flops 603979776 | bytes 7372800 | tf_op jit(solution)/shard_map/oi,ohw->ihw/dot_general | solution.py:64
  137.5 4.1 %fusion.121 = f32[8,256,768]{2,1,0:T(8,128)} fusion(bf16[192,10,258]{2,0,1:T(8,128)(2,1)S(1)} %fusion.42, bf16[3,3,192,768]{3,2,1,0:T(8,128)(2,1)S(1)} %copy-done.2), kind=kOutput, calls=%fused_computation.101 | convolution fusion | flops 603979776 | bytes 7372800 | tf_op jit(solution)/shard_map/oi,ohw->ihw/dot_general | solution.py:64
  141.5 3.8 %fusion.123 = f32[8,256,768]{2,1,0:T(8,128)} fusion(bf16[192,10,258]{2,0,1:T(8,128)(2,1)S(1)} %fusion.42, bf16[3,3,192,768]{3,2,1,0:T(8,128)(2,1)S(1)} %copy-done.2), kind=kOutput, calls=%fused_computation.103 | convolution fusion | flops 603979776 | bytes 7372800 | tf_op jit(solution)/shard_map/oi,ohw->ihw/dot_general | solution.py:64
  145.3 4.0 %fusion.125 = f32[8,256,768]{2,1,0:T(8,128)} fusion(bf16[192,10,258]{2,0,1:T(8,128)(2,1)S(1)} %fusion.42, bf16[3,3,192,768]{3,2,1,0:T(8,128)(2,1)S(1)} %copy-done.2), kind=kOutput, calls=%fused_computation.105 | convolution fusion | flops 603979776 | bytes 7372800 | tf_op jit(solution)/shard_map/oi,ohw->ihw/dot_general | solution.py:64
  149.3 3.7 %fusion.109 = f32[8,256,768]{2,1,0:T(8,128)} fusion(bf16[192,8,256]{2,0,1:T(8,128)(2,1)S(1)} %get-tuple-element.11, bf16[192,1,256]{2,0,1:T(8,128)(2,1)S(1)} %collective-permute-done.2, bf16[3,3,192,768]{3,2,1,0:T(8,128)(2,1)S(1)} %copy-done.2), kind=kOutput, calls=%fused_computation.88 | convolution fusion | flops 605749248 | bytes 7471104 | tf_op jit(solution)/shard_map/oi,ohw->ihw/dot_general | solution.py:64
  153.0 3.6 %fusion.105 = f32[8,256,768]{2,1,0:T(8,128)} fusion(bf16[192,1,256]{2,0,1:T(8,128)(2,1)S(1)} %collective-permute-done.3, bf16[192,8,256]{2,0,1:T(8,128)(2,1)S(1)} %get-tuple-element.11, bf16[3,3,192,768]{3,2,1,0:T(8,128)(2,1)S(1)} %copy-done.2), kind=kOutput, calls=%fused_computation.84 | convolution fusion | flops 605749248 | bytes 7471104 | tf_op jit(solution)/shard_map/oi,ohw->ihw/dot_general | solution.py:64
  156.6 19.0 %fusion.6 = bf16[768,8,256]{0,2,1:T(8,128)(2,1)} fusion(f32[8,256,768]{2,1,0:T(8,128)} %fusion.109, f32[8,256,768]{2,1,0:T(8,128)} %fusion.117, f32[8,256,768]{2,1,0:T(8,128)} %fusion.119, f32[8,256,768]{2,1,0:T(8,128)} %fusion.135, f32[8,256,768]{2,1,0:T(8,128)} %fusion.121, f32[8,256,768]{2,1,0:T(8,128)} %fusion.123, f32[8,256,768]{2,1,0:T(8,128)} %fusion.125, ...), kind=kOutput, calls=%fused_computation.11 | convolution fusion | flops 618135552 | bytes 54558720 | tf_op jit(solution)/shard_map/oi,ohw->ihw/dot_general | solution.py:64
  175.6 5.1 %copy.12 = bf16[768,8,256]{2,1,0:T(8,128)(2,1)} copy(bf16[768,8,256]{0,2,1:T(8,128)(2,1)} %fusion.6) | data formatting | bytes 6291456 | tf_op jit(solution)/shard_map/convert_element_type | solution.py:89
  181.9 1.3 copy.13
  183.2 9.8 %all-reduce.4.cloned.1.call-done = bf16[3,3,192,768]{3,2,1,0:T(8,128)(2,1)} async-done(((bf16[3,3,192,768]{3,2,1,0:T(8,128)(2,1)}), bf16[3,3,192,768]{3,2,1,0:T(8,128)(2,1)}) %all-reduce.4.cloned.1.call-update) | async-done | bytes 2654224 | tf_op jit(solution)/shard_map/psum | solution.py:92
  193.0 4.6 %convert_element_type.25 = f32[3,3,192,768]{3,2,1,0:T(8,128)} convert(bf16[3,3,192,768]{3,2,1,0:T(8,128)(2,1)} %all-reduce.4.cloned.1.call-done) | non-fusion elementwise | flops 1327104 | bytes 7962624 | tf_op jit(solution)/shard_map/convert_element_type | solution.py:92
  197.6 58.4 %reduce-scatter.2.cloned.1.call-done = bf16[192,8,256]{2,1,0:T(8,128)(2,1)} async-done(((bf16[768,8,256]{2,1,0:T(8,128)(2,1)}), bf16[192,8,256]{2,1,0:T(8,128)(2,1)}) %reduce-scatter.2.cloned.1.call-update) | async-done | bytes 786448 | tf_op jit(solution)/shard_map/reduce_scatter | solution.py:90
  (33 shorter events, 13.2 us)
Async XLA Ops:
  7.2 73.6 %copy-start.1 = (bf16[3,3,192,768]{3,2,1,0:T(8,128)(2,1)S(1)}, bf16[3,3,192,768]{3,2,1,0:T(8,128)(2,1)}, u32[]{:S(2)}) copy-start(bf16[3,3,192,768]{3,2,1,0:T(8,128)(2,1)} %param.4) | copy-start | bytes 7962628
  7.2 69.2 %all-gather.2.cloned.1.call-start = ((), (), s32[]{:S(2)}) async-start(), calls=%async_computation.1 | async-start | bytes 3932160 | tf_op jit(solution)/shard_map/all_gather | solution.py:78
  9.6 183.4 %all-reduce.4.cloned.1.call-start = ((), (), s32[]{:S(2)}) async-start(), calls=%async_computation.3 | async-start | bytes 5308416 | tf_op jit(solution)/shard_map/psum | solution.py:92
  76.3 7.9 %copy-start = (bf16[768,8,256]{2,0,1:T(8,128)(2,1)S(1)}, bf16[768,8,256]{2,0,1:T(8,128)(2,1)}, u32[]{:S(2)}) copy-start(bf16[768,8,256]{2,0,1:T(8,128)(2,1)} %all-gather.2.cloned.1.call-done) | copy-start | bytes 9437188
  77.7 5.8 %collective-permute-start = (bf16[768,1,256]{2,0,1:T(8,128)(2,1)S(1)}, bf16[768,1,256]{2,0,1:T(8,128)(2,1)S(1)}, u32[]{:S(2)}, u32[]{:S(2)}) collective-permute-start(bf16[768,1,256]{2,0,1:T(8,128)(2,1)S(1)} %get-tuple-element.9), channel_id=1, source_target_pairs={{0,4},{4,8},{8,12},{12,16},{16,20},{20,24},{24,28},{1,5},{5,9},{9,... | collective-permute-start | bytes 1179656 | tf_op jit(solution)/shard_map/ppermute | solution.py:14
  79.4 4.8 %collective-permute-start.1 = (bf16[768,1,256]{2,0,1:T(8,128)(2,1)S(1)}, bf16[768,1,256]{2,0,1:T(8,128)(2,1)S(1)}, u32[]{:S(2)}, u32[]{:S(2)}) collective-permute-start(bf16[768,1,256]{2,0,1:T(8,128)(2,1)S(1)} %get-tuple-element.10), channel_id=1, source_target_pairs={{4,0},{8,4},{12,8},{16,12},{20,16},{24,20},{28,24},{5,1},{9,5},{13... | collective-permute-start | bytes 1179656 | tf_op jit(solution)/shard_map/ppermute | solution.py:15
  94.0 1.1 copy-start.4
  110.6 17.2 %collective-permute-start.3 = (bf16[192,1,256]{2,0,1:T(8,128)(2,1)}, bf16[192,1,256]{2,0,1:T(8,128)(2,1)S(1)}, u32[]{:S(2)}, u32[]{:S(2)}) collective-permute-start(bf16[192,1,256]{2,0,1:T(8,128)(2,1)} %get-tuple-element.13), channel_id=1, source_target_pairs={{4,0},{8,4},{12,8},{16,12},{20,16},{24,20},{28,24},{5,1},{9,5},{13... | collective-permute-start | bytes 294920 | tf_op jit(solution)/shard_map/ppermute | solution.py:15
  111.9 16.0 %collective-permute-start.2 = (bf16[192,1,256]{2,0,1:T(8,128)(2,1)S(1)}, bf16[192,1,256]{2,0,1:T(8,128)(2,1)S(1)}, u32[]{:S(2)}, u32[]{:S(2)}) collective-permute-start(bf16[192,1,256]{2,0,1:T(8,128)(2,1)S(1)} %get-tuple-element.14), channel_id=1, source_target_pairs={{0,4},{4,8},{8,12},{12,16},{16,20},{20,24},{24,28},{1,5},{5,9},{9,... | collective-permute-start | bytes 294920 | tf_op jit(solution)/shard_map/ppermute | solution.py:14
  127.6 128.4 %reduce-scatter.2.cloned.1.call-start = ((), (), s32[]{:S(2)}) async-start(), calls=%async_computation.2 | async-start | bytes 3932160 | tf_op jit(solution)/shard_map/reduce_scatter | solution.py:90
  128.7 5.1 %copy-start.2 = (bf16[3,3,192,768]{3,2,1,0:T(8,128)(2,1)S(1)}, bf16[3,3,192,768]{3,2,1,0:T(8,128)(2,1)}, u32[]{:S(2)}) copy-start(bf16[3,3,192,768]{3,2,1,0:T(8,128)(2,1)} %param.4) | copy-start | bytes 7962628
  180.7 1.2 copy-start.3
Sparse Core Ops, SparseCore 0:
  10.2 66.1 all-gather.1
  127.7 65.2 all-reduce.3
  196.0 59.9 reduce-scatter.1

commit v2 on v1

v2 whole, which is shorter than its diff:
```python
import functools

import jax
import jax.numpy as jnp
from jax import lax
from jax.experimental import pallas as pl
from jax.experimental.pallas import tpu as pltpu
from jax.sharding import PartitionSpec as P

BF = jnp.bfloat16
F32 = jnp.float32
MESH = pl.DeviceIdType.MESH
CHUNKS = 2


def shifted(value, by):
    width = value.shape[1]
    col = lax.broadcasted_iota(jnp.int32, value.shape, 1)
    edge = width - 1 if by == 1 else 0
    return jnp.where(col == edge, 0.0, pltpu.roll(value, (-by) % width, 1))


def kernel(
    n, S, x_ref, ct_ref, wb_ref, wt_ref, act_ref, ig_ref, wg_ref,
    frame, acc, grads, sbuf, rbuf, part, pair_buf, chip_buf,
    own_sem, gs_sem, gr_sem, hs_sem, hr_sem, es_sem, er_sem, rs_sem, rr_sem,
    ps_sem, pr_sem, cs_sem, cr_sem, as_sem, ar_sem, fs_sem, fr_sem,
):
    R, Cb, W = x_ref.shape
    O = ct_ref.shape[1]
    T = 3 * O
    G = S // 2
    half = R // CHUNKS
    s = lax.axis_index("space")
    c = lax.axis_index("chan")

    barrier = pltpu.get_barrier_semaphore()
    for k in range(1, S):
        pl.semaphore_signal(barrier, 1, device_id=(lax.rem(s + k, S), c), device_id_type=MESH)

    @pl.when(c > 0)
    def _():
        pl.semaphore_signal(barrier, 1, device_id=(s, c - 1), device_id_type=MESH)

    @pl.when(c < n - 1)
    def _():
        pl.semaphore_signal(barrier, 1, device_id=(s, c + 1), device_id_type=MESH)

    own = pltpu.make_async_copy(x_ref, frame.at[c, pl.ds(1, R)], own_sem)
    own.start()
    zero_row = jnp.zeros((Cb, W), BF)

    @pl.when(s == 0)
    def _():
        for j in range(n):
            frame[j, 0] = zero_row
        grads[0] = jnp.zeros((T, W), BF)

    @pl.when(s == S - 1)
    def _():
        for j in range(n):
            frame[j, R + 1] = zero_row
        grads[R + 1] = jnp.zeros((T, W), BF)

    acc[...] = jnp.zeros_like(acc)
    pl.semaphore_wait(barrier, S - 1 + jnp.minimum(c, 1) + jnp.minimum(n - 1 - c, 1))
    own.wait()

    def peer(way):
        return (s, c + 1) if way == 0 else (s, c - 1)

    def gather_copy(way, step, part_no, block):
        rows = pl.ds(1 + part_no * half, half)
        return pltpu.make_async_remote_copy(
            src_ref=frame.at[block, rows], dst_ref=frame.at[block, rows],
            send_sem=gs_sem.at[way, step, part_no], recv_sem=gr_sem.at[way, step, part_no],
            device_id=peer(way), device_id_type=MESH,
        )

    def sends(way, step):
        if way == 0:
            return c - step, jnp.logical_and(c - step >= 0, c < n - 1)
        return c + step, jnp.logical_and(c + step <= n - 1, c > 0)

    def receives(way, step):
        if way == 0:
            return c - 1 - step, c - 1 - step >= 0
        return c + 1 + step, c + 1 + step <= n - 1

    def halo_copy(slot, side, block):
        src, dst, to = (R, 0, s + 1) if side == 0 else (1, R + 1, s - 1)
        return pltpu.make_async_remote_copy(
            src_ref=frame.at[block, src], dst_ref=frame.at[block, dst],
            send_sem=hs_sem.at[slot, side], recv_sem=hr_sem.at[slot, side],
            device_id=(to, c), device_id_type=MESH,
        )

    def halo_start(slot, block):
        @pl.when(s < S - 1)
        def _():
            halo_copy(slot, 0, block).start()

        @pl.when(s > 0)
        def _():
            halo_copy(slot, 1, block).start()

    def halo_wait(slot, block):
        @pl.when(s < S - 1)
        def _():
            halo_copy(slot, 0, block).wait_send()
            halo_copy(slot, 1, block).wait_recv()

        @pl.when(s > 0)
        def _():
            halo_copy(slot, 1, block).wait_send()
            halo_copy(slot, 0, block).wait_recv()

    def forward(block):
        def row(h, carry):
            total = acc[h]
            for a in range(3):
                total = total + jnp.dot(wb_ref[block, a], frame[block, h + a], preferred_element_type=F32)
            acc[h] = total
            return carry

        lax.fori_loop(0, R, row, 0)

    def start_gather(step, part_no):
        for way in range(2):
            block, valid = sends(way, step)

            @pl.when(valid)
            def _():
                gather_copy(way, step, part_no, block).start()

    for p in range(CHUNKS):
        start_gather(0, p)
    halo_start(0, c)
    halo_wait(0, c)
    forward(c)
    for step in range(n - 1):
        for p in range(CHUNKS):
            for way in range(2):
                block, valid = receives(way, step)

                @pl.when(valid)
                def _():
                    gather_copy(way, step, p, block).wait_recv()

            if step < n - 2:
                start_gather(step + 1, p)
        for way in range(2):
            block, valid = receives(way, step)

            @pl.when(valid)
            def _():
                halo_start(1 + 2 * step + way, block)
        for way in range(2):
            block, valid = receives(way, step)

            @pl.when(valid)
            def _():
                halo_wait(1 + 2 * step + way, block)
                forward(block)

    def activate(h):
        pre = shifted(acc[h, :O], -1) + acc[h, O : 2 * O] + shifted(acc[h, 2 * O :], 1)
        sigma = jax.nn.sigmoid(pre)
        act_ref[h] = (pre * sigma).astype(BF)
        grad = (ct_ref[h].astype(F32) * sigma * (1.0 + pre * (1.0 - sigma))).astype(BF)
        wide = grad.astype(F32)
        grads[h + 1, :O] = shifted(wide, 1).astype(BF)
        grads[h + 1, O : 2 * O] = grad
        grads[h + 1, 2 * O :] = shifted(wide, -1).astype(BF)

    def edge_copy(side):
        src, dst, to = (R, 0, s + 1) if side == 0 else (1, R + 1, s - 1)
        return pltpu.make_async_remote_copy(
            src_ref=grads.at[src], dst_ref=grads.at[dst],
            send_sem=es_sem.at[side], recv_sem=er_sem.at[side],
            device_id=(to, c), device_id_type=MESH,
        )

    def edges(k, carry):
        activate(k * (R - 1))
        return carry

    lax.fori_loop(0, 2, edges, 0)

    @pl.when(s < S - 1)
    def _():
        edge_copy(0).start()

    @pl.when(s > 0)
    def _():
        edge_copy(1).start()

    def middle(h, carry):
        activate(h)
        return carry

    lax.fori_loop(1, R - 1, middle, 0)

    @pl.when(s < S - 1)
    def _():
        edge_copy(0).wait_send()
        edge_copy(1).wait_recv()

    @pl.when(s > 0)
    def _():
        edge_copy(1).wait_send()
        edge_copy(0).wait_recv()

    def own_row(block, h):
        total = jnp.dot(wt_ref[block, 0], grads[h + 2], preferred_element_type=F32)
        total = total + jnp.dot(wt_ref[block, 1], grads[h + 1], preferred_element_type=F32)
        return total + jnp.dot(wt_ref[block, 2], grads[h], preferred_element_type=F32)

    def scatter_dest(way, step):
        far = n - 1 - step
        if way == 0:
            return c + far, c + far <= n - 1
        return c - far, c - far >= 0

    def scatter_arrives(way, step):
        far = n - 1 - step
        if way == 0:
            return jnp.logical_and(c >= 1, c - 1 + far <= n - 1)
        return jnp.logical_and(c <= n - 2, c + 1 - far >= 0)

    def scatter_copy(way, step, part_no):
        rows = pl.ds(part_no * half, half)
        return pltpu.make_async_remote_copy(
            src_ref=sbuf.at[way, step, rows], dst_ref=rbuf.at[way, step, rows],
            send_sem=rs_sem.at[way, step, part_no], recv_sem=rr_sem.at[way, step, part_no],
            device_id=peer(way), device_id_type=MESH,
        )

    def scatter_own(step, part_no):
        for way in range(2):
            dest, valid = scatter_dest(way, step)

            @pl.when(valid)
            def _():
                def row(h, carry):
                    sbuf[way, step, h] = own_row(dest, h).astype(BF)
                    return carry

                lax.fori_loop(part_no * half, (part_no + 1) * half, row, 0)

    def scatter_send(step, part_no):
        for way in range(2):
            _, valid = scatter_dest(way, step)
            if step > 0:
                arrived = scatter_arrives(way, step - 1)

                @pl.when(arrived)
                def _():
                    scatter_copy(way, step - 1, part_no).wait_recv()

                    def row(h, carry):
                        total = sbuf[way, step, h].astype(F32) + rbuf[way, step - 1, h].astype(F32)
                        sbuf[way, step, h] = total.astype(BF)
                        return carry

                    lax.fori_loop(part_no * half, (part_no + 1) * half, row, 0)

            @pl.when(valid)
            def _():
                scatter_copy(way, step, part_no).start()

    def wgrad(block):
        def tap(a, carry):
            total = jnp.zeros((T, Cb), F32)
            for h in range(R):
                total = total + lax.dot_general(
                    grads[h + 1], frame[block, h + a], (((1,), (1,)), ((), ())),
                    preferred_element_type=F32,
                )
            start = pl.multiple_of((block * 3 + a) * T, 16)
            part[pl.ds(start, T)] = total.astype(BF)
            return carry

        lax.fori_loop(0, 3, tap, 0)

    rows_all = part.shape[0]
    rows_half = rows_all // 2
    piece = rows_half // G
    side = lax.rem(s, 2)
    chip = lax.div(s, 2)
    mate = (s + 1 - 2 * side, c)
    mine = side * rows_half
    theirs = (1 - side) * rows_half

    def span(start, size):
        return pl.ds(pl.multiple_of(start, 16), size)

    def pair_copy():
        return pltpu.make_async_remote_copy(
            src_ref=part.at[span(theirs, rows_half)], dst_ref=pair_buf,
            send_sem=ps_sem, recv_sem=pr_sem, device_id=mate, device_id_type=MESH,
        )

    def chip_copy(k):
        to = lax.rem(chip + k, G)
        return pltpu.make_async_remote_copy(
            src_ref=part.at[span(mine + to * piece, piece)], dst_ref=chip_buf.at[k - 1],
            send_sem=cs_sem.at[k - 1], recv_sem=cr_sem.at[k - 1],
            device_id=(2 * to + side, c), device_id_type=MESH,
        )

    def share_copy(k):
        to = lax.rem(chip + k, G)
        rows = span(mine + chip * piece, piece)
        return pltpu.make_async_remote_copy(
            src_ref=wg_ref.at[rows], dst_ref=wg_ref.at[rows],
            send_sem=as_sem.at[k - 1], recv_sem=ar_sem.at[k - 1],
            device_id=(2 * to + side, c), device_id_type=MESH,
        )

    def mate_copy(k):
        origin = lax.rem(chip - k + G, G)
        rows = span(mine + origin * piece, piece)
        return pltpu.make_async_remote_copy(
            src_ref=wg_ref.at[rows], dst_ref=wg_ref.at[rows],
            send_sem=fs_sem.at[k], recv_sem=fr_sem.at[k],
            device_id=mate, device_id_type=MESH,
        )

    def reduce_stage(stage):
        if stage == 0:
            pair_copy().start()
        elif stage == 1:
            pair_copy().wait()

            def add(i, carry):
                rows = span(mine + i * 16, 16)
                got = pair_buf[span(i * 16, 16)].astype(F32)
                part[rows] = (part[rows].astype(F32) + got).astype(BF)
                return carry

            lax.fori_loop(0, rows_half // 16, add, 0, unroll=6)
            for k in range(1, G):
                chip_copy(k).start()
        elif stage == 2:
            for k in range(1, G):
                chip_copy(k).wait()

            def add(i, carry):
                rows = span(mine + chip * piece + i * 16, 16)
                total = part[rows].astype(F32)
                for k in range(1, G):
                    total = total + chip_buf[k - 1, span(i * 16, 16)].astype(F32)
                wg_ref[rows] = total.astype(BF)
                return carry

            lax.fori_loop(0, piece // 16, add, 0, unroll=3)
            for k in range(1, G):
                share_copy(k).start()
            mate_copy(0).start()
        else:
            for k in range(1, G):
                share_copy(k).wait()
                mate_copy(k).start()

    for p in range(CHUNKS):
        scatter_own(0, p)
        scatter_send(0, p)

    def all_wgrad(block, carry):
        wgrad(block)
        return carry

    lax.fori_loop(0, n, all_wgrad, 0)
    reduce_stage(0)
    stage = 1
    for step in range(1, n):
        if step < n - 1:
            for p in range(CHUNKS):
                scatter_own(step, p)
            if stage < 2:
                reduce_stage(stage)
                stage += 1
            for p in range(CHUNKS):
                scatter_send(step, p)
        else:
            def row(h, carry):
                acc[h, :Cb] = own_row(c, h)
                return carry

            lax.fori_loop(0, R, row, 0)
    while stage < 4:
        reduce_stage(stage)
        stage += 1

    for way in range(2):
        arrived = scatter_arrives(way, n - 2)

        @pl.when(arrived)
        def _():
            for p in range(CHUNKS):
                scatter_copy(way, n - 2, p).wait_recv()

            def row(h, carry):
                acc[h, :Cb] = acc[h, :Cb] + rbuf[way, n - 2, h].astype(F32)
                return carry

            lax.fori_loop(0, R, row, 0)

    def last(h, carry):
        ig_ref[h] = acc[h, :Cb].astype(BF)
        return carry

    lax.fori_loop(0, R, last, 0)

    for k in range(G):
        mate_copy(k).wait()
    for step in range(n - 1):
        for way in range(2):
            block, valid = sends(way, step)
            _, out = scatter_dest(way, step)

            @pl.when(valid)
            def _():
                for p in range(CHUNKS):
                    gather_copy(way, step, p, block).wait_send()

            @pl.when(out)
            def _():
                for p in range(CHUNKS):
                    scatter_copy(way, step, p).wait_send()


def on_device(n, S, images, weight, cotangent):
    Cb, R, W = images.shape
    O = weight.shape[2]
    T = 3 * O
    x = images.transpose(1, 0, 2)
    ct = cotangent.transpose(1, 0, 2)
    w = weight.reshape(3, 3, O, n, Cb)
    wb = w.transpose(3, 0, 1, 2, 4).reshape(n, 3, T, Cb)
    wt = w.transpose(3, 0, 4, 1, 2).reshape(n, 3, Cb, T)
    rows_all = n * 3 * T
    dma = pltpu.SemaphoreType.DMA
    vmem = pl.BlockSpec(memory_space=pltpu.VMEM)
    act, ig, wg = pl.pallas_call(
        functools.partial(kernel, n, S),
        out_shape=(
            jax.ShapeDtypeStruct((R, O, W), BF),
            jax.ShapeDtypeStruct((R, Cb, W), BF),
            jax.ShapeDtypeStruct((rows_all, Cb), BF),
        ),
        in_specs=[vmem] * 4,
        out_specs=(vmem, vmem, vmem),
        scratch_shapes=[
            pltpu.VMEM((n, R + 2, Cb, W), BF),
            pltpu.VMEM((R, T, W), F32),
            pltpu.VMEM((R + 2, T, W), BF),
            pltpu.VMEM((2, n - 1, R, Cb, W), BF),
            pltpu.VMEM((2, n - 1, R, Cb, W), BF),
            pltpu.VMEM((rows_all, Cb), BF),
            pltpu.VMEM((rows_all // 2, Cb), BF),
            pltpu.VMEM((S // 2 - 1, rows_all // S, Cb), BF),
            dma,
            dma((2, n - 1, CHUNKS)), dma((2, n - 1, CHUNKS)),
            dma((2 * n - 1, 2)), dma((2 * n - 1, 2)),
            dma((2,)), dma((2,)),
            dma((2, n - 1, CHUNKS)), dma((2, n - 1, CHUNKS)),
            dma, dma,
            dma((S // 2 - 1,)), dma((S // 2 - 1,)),
            dma((S // 2 - 1,)), dma((S // 2 - 1,)),
            dma((S // 2,)), dma((S // 2,)),
        ],
        compiler_params=pltpu.CompilerParams(
            collective_id=0, has_side_effects=True, vmem_limit_bytes=60 * 2**20
        ),
    )(x, ct, wb, wt)
    weight_grad = wg.astype(F32).reshape(n, 3, 3, O, Cb).transpose(1, 2, 3, 0, 4)
    return (
        act.transpose(1, 0, 2),
        ig.transpose(1, 0, 2),
        weight_grad.reshape(3, 3, O, n * Cb),
    )


def solution(mesh):
    return jax.shard_map(
        functools.partial(on_device, mesh.shape["chan"], mesh.shape["space"]),
        mesh=mesh,
        in_specs=(P("chan", "space", None), P(None, None, "chan", None), P("chan", "space", None)),
        out_specs=(P("chan", "space", None), P("chan", "space", None), P(None, None, "chan", None)),
        check_vma=False,
    )
```

time: 263 us -> 179 us (0.68)
  Pallas kernels: 0 us -> 140 us
  waiting for transfers between devices: 136 us -> 0 us
  matrix products: 74.3 us -> 0 us
  local copies, waits for them, and re-layouts: 12.2 us -> 34.6 us
  starting transfers between devices: 14.6 us -> 0 us
  between operations: 14 us -> 0.68 us
  other arithmetic: 11.5 us -> 2.88 us
    pallas_call x0 -> x1, Pallas kernels: none -> 140 us  [on_device(): pl.pallas_call(functools.partial(kernel, n, S), out_shape=(jax.ShapeDtype...]
    dot_general x27 -> x0, matrix products: 74.3 us -> none  [the longest x9 50.6 us: transpose_taps(): jnp.einsum('oi,ohw->ihw', kernel[row_tap, col_tap], wide[:, 2 - row_tap:2...]
    all_gather x1 -> x0, waiting for transfers between devices: 66.7 us -> none  [on_device(): gathered = lax.all_gather(images, 'chan', axis=0, tiled=True)]
    reduce_scatter x1 -> x0, waiting for transfers between devices: 58.4 us -> none  [on_device(): lax.psum_scatter(partial, 'chan', scatter_dimension=0, tiled=True)]
    reshape x0 -> x5, local copies, waits for them, and re-layouts: none -> 26.7 us  [the longest x2 15.9 us: on_device(): weight_grad.reshape(3, 3, O, n * Cb)]
    ppermute x4 -> x0, starting transfers between devices: 14.3 us -> none  [the longest x2 11.7 us: with_halo(): before = lax.ppermute(last, axis, up)]
    psum x1 -> x0, waiting for transfers between devices: 9.79 us -> none  [on_device(): weight_grad = lax.psum(local_wgrad, 'space').astype(jnp.float32)]
    convert_element_type x1 -> x0, local copies, waits for them, and re-layouts: 5.11 us -> none  [on_device(): transpose_taps(weight, grad_wide, rows, width).astype(jnp.bfloat16)]
  transfers between devices with their start and end apart: 7 -> 0, of which waited for: 4 -> 0; matrix products, arithmetic and copies ran while one was open for 26% -> 0% of each run, Pallas kernels for 0% -> 0%
where the time goes in v2:
time: 179 us; the launch traced here: 178 us
  Pallas kernels  140 us (78%)
  local copies, waits for them, and re-layouts  34.6 us (19%)
  other arithmetic  2.88 us (2%)
    pallas_call x1, Pallas kernels, on_device(): pl.pallas_call(functools.partial(kernel, n, S), out_shape=(jax.ShapeDtype...  140 us
    reshape x2, local copies, waits for them, and re-layouts, on_device(): weight_grad.reshape(3, 3, O, n * Cb)  15.9 us
    reshape x2, local copies, waits for them, and re-layouts, on_device(): w = weight.reshape(3, 3, O, n, Cb)  6.75 us
    unnamed x6, local copies, waits for them, and re-layouts  4.91 us
    reshape x1, local copies, waits for them, and re-layouts, on_device(): wt = w.transpose(3, 0, 4, 1, 2).reshape(n, 3, Cb, T)  4.05 us

profile of v2, /device:TPU:0, one launch (start us, length us, event | category | flops | bytes accessed | tf_op | source)
XLA Modules:
  0.0 178.4 jit_solution(7053327302885102722)
XLA Ops:
  0.6 0.0 copy-start.1
  0.6 3.0 %copy_bitcast_fusion = (bf16[8,192,256]{2,1,0:T(8,128)(2,1)}, bf16[8,192,256]{2,1,0:T(8,128)(2,1)}) fusion(bf16[192,8,256]{2,1,0:T(8,128)(2,1)} %param.5, bf16[192,8,256]{2,1,0:T(8,128)(2,1)} %param.3), kind=kLoop, calls=%fused_computation.1 | loop fusion | bytes 3145728 | tf_op jit(solution)/shard_map/transpose | solution.py:439
  3.7 0.0 copy-done.1
  3.7 4.1 %reshape.25 = bf16[3,3,192,4,192]{4,3,2,1,0:T(4,128)(2,1)} reshape(bf16[3,3,192,768]{3,2,1,0:T(8,128)(2,1)S(1)} %copy-done.1) | data formatting | bytes 5308416 | tf_op jit(solution)/shard_map/reshape | solution.py:440
  7.8 2.6 %copy.15 = bf16[3,3,192,4,192]{4,2,1,0,3:T(8,128)(2,1)S(1)} copy(bf16[3,3,192,4,192]{4,3,2,1,0:T(4,128)(2,1)} %reshape.25) | data formatting | bytes 5308416 | tf_op jit(solution)/shard_map/reshape | solution.py:440
  10.4 0.0 copy-start
  10.4 4.0 %copy.17.wt_ref = bf16[4,3,192,576]{3,2,1,0:T(8,128)(2,1)} copy(bf16[4,3,192,576]{2,3,1,0:T(8,128)(2,1)S(1)} %bitcast.18) | data formatting | bytes 5308416 | tf_op jit(solution)/shard_map/reshape | solution.py:442
  14.5 0.0 copy-done
  14.5 140.2 %shard_map.58 = (bf16[8,192,256]{2,1,0:T(8,128)(2,1)}, bf16[8,192,256]{2,1,0:T(8,128)(2,1)}, bf16[6912,192]{1,0:T(8,128)(2,1)}) custom-call(bf16[8,192,256]{2,1,0:T(8,128)(2,1)} %get-tuple-element.16.x_ref, bf16[8,192,256]{2,1,0:T(8,128)(2,1)} %get-tuple-element.15.ct_ref, bf16[4,3,576,192]{3,2,1,0:T(8,128)(2,1)} %bitcast.19, ...), custom_call_target="tpu_custom_call" | custom-call | tf_op jit(solution)/shard_map/pallas_call | solution.py:446
  154.7 2.4 %copy.19 = bf16[192,8,256]{2,1,0:T(8,128)(2,1)} copy(bf16[192,8,256]{2,0,1:T(8,128)(2,1)} %bitcast.22) | data formatting | bytes 1572864
  157.2 2.4 %copy.20 = bf16[192,8,256]{2,1,0:T(8,128)(2,1)} copy(bf16[192,8,256]{2,0,1:T(8,128)(2,1)} %bitcast.21) | data formatting | bytes 1572864
  159.6 2.9 %convert_bitcast_fusion = f32[3,3,192,4,192]{4,2,1,0,3:T(8,128)S(1)} fusion(bf16[4,3,3,192,192]{4,3,2,1,0:T(8,128)(2,1)} %bitcast.20), kind=kLoop, calls=%fused_computation | loop fusion | flops 1327104 | bytes 7962624 | tf_op jit(solution)/shard_map/reshape | solution.py:482
  162.5 7.5 %copy.18 = f32[3,3,192,4,192]{4,3,2,1,0:T(4,128)} copy(f32[3,3,192,4,192]{4,2,1,0,3:T(8,128)S(1)} %convert_bitcast_fusion) | data formatting | bytes 10616832 | tf_op jit(solution)/shard_map/reshape | solution.py:482
  170.0 8.4 %reshape.32 = f32[3,3,192,768]{3,2,1,0:T(8,128)} reshape(f32[3,3,192,4,192]{4,3,2,1,0:T(4,128)} %copy.18) | data formatting | bytes 10616832 | tf_op jit(solution)/shard_map/reshape | solution.py:482
Async XLA Ops:
  0.6 3.0 %copy-start.1 = (bf16[3,3,192,768]{3,2,1,0:T(8,128)(2,1)S(1)}, bf16[3,3,192,768]{3,2,1,0:T(8,128)(2,1)}, u32[]{:S(2)}) copy-start(bf16[3,3,192,768]{3,2,1,0:T(8,128)(2,1)} %param.4) | copy-start | bytes 7962628
  10.4 4.1 %copy-start = (bf16[3,3,192,4,192]{4,2,1,0,3:T(8,128)(2,1)}, bf16[3,3,192,4,192]{4,2,1,0,3:T(8,128)(2,1)S(1)}, u32[]{:S(2)}) copy-start(bf16[3,3,192,4,192]{4,2,1,0,3:T(8,128)(2,1)S(1)} %copy.15) | copy-start | bytes 7962628

commit v3 on v2

--- a/solution.py
+++ b/solution.py
@@ -21,8 +21,8 @@
 
 
 def kernel(
-    n, S, x_ref, ct_ref, wb_ref, wt_ref, act_ref, ig_ref, wg_ref,
-    frame, acc, grads, sbuf, rbuf, part, pair_buf, chip_buf,
+    n, S, x_ref, ct_ref, w_ref, act_ref, ig_ref, wg_ref,
+    wb_ref, wt_ref, frame, acc, grads, sbuf, rbuf, part, pair_buf, chip_buf,
     own_sem, gs_sem, gr_sem, hs_sem, hr_sem, es_sem, er_sem, rs_sem, rr_sem,
     ps_sem, pr_sem, cs_sem, cr_sem, as_sem, ar_sem, fs_sem, fr_sem,
 ):
@@ -136,8 +136,24 @@
     for p in range(CHUNKS):
         start_gather(0, p)
     halo_start(0, c)
+
+    def cut(a, carry):
+        for b in range(3):
+            whole = w_ref[3 * a + b]
+            for j in range(n):
+                wb_ref[j, a, b * O : (b + 1) * O] = whole[:, j * Cb : (j + 1) * Cb]
+        return carry
+
+    lax.fori_loop(0, 3, cut, 0)
     halo_wait(0, c)
     forward(c)
+
+    def turn(k, carry):
+        j, a = lax.div(k, 3), lax.rem(k, 3)
+        wt_ref[j, a] = wb_ref[j, a].T
+        return carry
+
+    lax.fori_loop(0, 3 * n, turn, 0)
     for step in range(n - 1):
         for p in range(CHUNKS):
             for way in range(2):
@@ -269,19 +285,25 @@
             def _():
                 scatter_copy(way, step, part_no).start()
 
-    def wgrad(block):
-        def tap(a, carry):
-            total = jnp.zeros((T, Cb), F32)
-            for h in range(R):
-                total = total + lax.dot_general(
-                    grads[h + 1], frame[block, h + a], (((1,), (1,)), ((), ())),
-                    preferred_element_type=F32,
-                )
-            start = pl.multiple_of((block * 3 + a) * T, 16)
-            part[pl.ds(start, T)] = total.astype(BF)
-            return carry
-
-        lax.fori_loop(0, 3, tap, 0)
+    taps = 9 * O
+    lanes = n * Cb // 128
+
+    def wgrad(k, carry):
+        a, b = lax.div(k, 3), lax.rem(k, 3)
+        total = jnp.zeros((O, n * Cb), F32)
+        for h in range(R):
+            rows = jnp.concatenate([frame[j, h + a] for j in range(n)], axis=0)
+            total = total + lax.dot_general(
+                grads[h + 1, pl.ds(pl.multiple_of(b * O, 16), O)], rows, (((1,), (1,)), ((), ())),
+                preferred_element_type=F32,
+            )
+        for q in range(lanes):
+            start = pl.multiple_of(q * taps + k * O, 16)
+            part[pl.ds(start, O)] = total[:, q * 128 : (q + 1) * 128].astype(BF)
+        return carry
+
+    if part.shape[0] > lanes * taps:
+        part[lanes * taps :] = jnp.zeros((part.shape[0] - lanes * taps, 128), BF)
 
     rows_all = part.shape[0]
     rows_half = rows_all // 2
@@ -334,27 +356,23 @@
             pair_copy().wait()
 
             def add(i, carry):
-                rows = span(mine + i * 16, 16)
-                got = pair_buf[span(i * 16, 16)].astype(F32)
+                rows = span(mine + i * piece, piece)
+                got = pair_buf[span(i * piece, piece)].astype(F32)
                 part[rows] = (part[rows].astype(F32) + got).astype(BF)
                 return carry
 
-            lax.fori_loop(0, rows_half // 16, add, 0, unroll=6)
+            lax.fori_loop(0, G, add, 0)
             for k in range(1, G):
                 chip_copy(k).start()
         elif stage == 2:
             for k in range(1, G):
                 chip_copy(k).wait()
 
-            def add(i, carry):
-                rows = span(mine + chip * piece + i * 16, 16)
-                total = part[rows].astype(F32)
-                for k in range(1, G):
-                    total = total + chip_buf[k - 1, span(i * 16, 16)].astype(F32)
-                wg_ref[rows] = total.astype(BF)
-                return carry
-
-            lax.fori_loop(0, piece // 16, add, 0, unroll=3)
+            rows = span(mine + chip * piece, piece)
+            total = part[rows].astype(F32)
+            for k in range(1, G):
+                total = total + chip_buf[k - 1].astype(F32)
+            wg_ref[rows] = total.astype(BF)
             for k in range(1, G):
                 share_copy(k).start()
             mate_copy(0).start()
@@ -367,28 +385,26 @@
         scatter_own(0, p)
         scatter_send(0, p)
 
-    def all_wgrad(block, carry):
-        wgrad(block)
-        return carry
-
-    lax.fori_loop(0, n, all_wgrad, 0)
+    lax.fori_loop(0, 9, wgrad, 0)
     reduce_stage(0)
     stage = 1
-    for step in range(1, n):
-        if step < n - 1:
-            for p in range(CHUNKS):
-                scatter_own(step, p)
-            if stage < 2:
-                reduce_stage(stage)
-                stage += 1
-            for p in range(CHUNKS):
-                scatter_send(step, p)
-        else:
-            def row(h, carry):
-                acc[h, :Cb] = own_row(c, h)
-                return carry
-
-            lax.fori_loop(0, R, row, 0)
+    for step in range(1, n - 1):
+        for p in range(CHUNKS):
+            scatter_own(step, p)
+        if stage == 1:
+            reduce_stage(stage)
+            stage += 1
+        for p in range(CHUNKS):
+            scatter_send(step, p)
+        if step == 2:
+            reduce_stage(stage)
+            stage += 1
+
+    def row(h, carry):
+        acc[h, :Cb] = own_row(c, h)
+        return carry
+
+    lax.fori_loop(0, R, row, 0)
     while stage < 4:
         reduce_stage(stage)
         stage += 1
@@ -431,16 +447,21 @@
                     scatter_copy(way, step, p).wait_send()
 
 
+def widen_kernel(in_ref, out_ref):
+    for q in range(in_ref.shape[0]):
+        out_ref[:, q * 128 : (q + 1) * 128] = in_ref[q].astype(F32)
+
+
 def on_device(n, S, images, weight, cotangent):
     Cb, R, W = images.shape
     O = weight.shape[2]
     T = 3 * O
     x = images.transpose(1, 0, 2)
     ct = cotangent.transpose(1, 0, 2)
-    w = weight.reshape(3, 3, O, n, Cb)
-    wb = w.transpose(3, 0, 1, 2, 4).reshape(n, 3, T, Cb)
-    wt = w.transpose(3, 0, 4, 1, 2).reshape(n, 3, Cb, T)
-    rows_all = n * 3 * T
+    w = weight.reshape(9, O, n * Cb)
+    lanes = n * Cb // 128
+    rows = lanes * 9 * O
+    rows_all = -(-rows // (16 * S)) * 16 * S
     dma = pltpu.SemaphoreType.DMA
     vmem = pl.BlockSpec(memory_space=pltpu.VMEM)
     act, ig, wg = pl.pallas_call(
@@ -448,19 +469,21 @@
         out_shape=(
             jax.ShapeDtypeStruct((R, O, W), BF),
             jax.ShapeDtypeStruct((R, Cb, W), BF),
-            jax.ShapeDtypeStruct((rows_all, Cb), BF),
+            jax.ShapeDtypeStruct((rows_all, 128), BF),
         ),
-        in_specs=[vmem] * 4,
+        in_specs=[vmem] * 3,
         out_specs=(vmem, vmem, vmem),
         scratch_shapes=[
+            pltpu.VMEM((n, 3, T, Cb), BF),
+            pltpu.VMEM((n, 3, Cb, T), BF),
             pltpu.VMEM((n, R + 2, Cb, W), BF),
             pltpu.VMEM((R, T, W), F32),
             pltpu.VMEM((R + 2, T, W), BF),
             pltpu.VMEM((2, n - 1, R, Cb, W), BF),
             pltpu.VMEM((2, n - 1, R, Cb, W), BF),
-            pltpu.VMEM((rows_all, Cb), BF),
-            pltpu.VMEM((rows_all // 2, Cb), BF),
-            pltpu.VMEM((S // 2 - 1, rows_all // S, Cb), BF),
+            pltpu.VMEM((rows_all, 128), BF),
+            pltpu.VMEM((rows_all // 2, 128), BF),
+            pltpu.VMEM((S // 2 - 1, rows_all // S, 128), BF),
             dma,
             dma((2, n - 1, CHUNKS)), dma((2, n - 1, CHUNKS)),
             dma((2 * n - 1, 2)), dma((2 * n - 1, 2)),
@@ -474,8 +497,15 @@
         compiler_params=pltpu.CompilerParams(
             collective_id=0, has_side_effects=True, vmem_limit_bytes=60 * 2**20
         ),
-    )(x, ct, wb, wt)
-    weight_grad = wg.astype(F32).reshape(n, 3, 3, O, Cb).transpose(1, 2, 3, 0, 4)
+    )(x, ct, w)
+    wg = wg[:rows].reshape(lanes, 9 * O, 128)
+    weight_grad = pl.pallas_call(
+        widen_kernel,
+        grid=(9,),
+        in_specs=[pl.BlockSpec((lanes, O, 128), lambda k: (0, k, 0))],
+        out_specs=pl.BlockSpec((O, n * Cb), lambda k: (k, 0)),
+        out_shape=jax.ShapeDtypeStruct((9 * O, n * Cb), F32),
+    )(wg)
     return (
         act.transpose(1, 0, 2),
         ig.transpose(1, 0, 2),

time: 179 us -> 146 us (0.82)
  local copies, waits for them, and re-layouts: 34.6 us -> 7.75 us
  Pallas kernels: 140 us -> 135 us
  other arithmetic: 2.88 us -> 0 us
    reshape x5 -> x0, local copies, waits for them, and re-layouts: 26.7 us -> none  [the longest x2 15.9 us: on_device(): weight_grad.reshape(3, 3, O, n * Cb)]
    pallas_call x1, Pallas kernels: 140 us -> 129 us  [on_device(): pl.pallas_call(functools.partial(kernel, n, S), out_shape=(jax.ShapeDtype...]
    pallas_call x0 -> x1, Pallas kernels: none -> 6.79 us  [on_device(): pl.pallas_call(widen_kernel, grid=(9,), in_specs=[pl.BlockSpec((lanes, O,...]
    reshape x1 -> x0, other arithmetic: 2.88 us -> none  [on_device(): weight_grad.reshape(3, 3, O, n * Cb)]
    unnamed x6 -> x2, local copies, waits for them, and re-layouts: 4.91 us -> 4.9 us
where the time goes in v3:
time: 146 us; the launch traced here: 144 us
  Pallas kernels  135 us (92%)
  local copies, waits for them, and re-layouts  7.75 us (5%)
    pallas_call x1, Pallas kernels, on_device(): pl.pallas_call(functools.partial(kernel, n, S), out_shape=(jax.ShapeDtype...  129 us
    pallas_call x1, Pallas kernels, on_device(): pl.pallas_call(widen_kernel, grid=(9,), in_specs=[pl.BlockSpec((lanes, O,...  6.79 us
    unnamed x2, local copies, waits for them, and re-layouts  4.9 us

profile of v3, /device:TPU:0, one launch (start us, length us, event | category | flops | bytes accessed | tf_op | source)
XLA Modules:
  0.0 143.7 jit_solution(4034704578972310427)
XLA Ops:
  0.6 2.9 %copy_bitcast_fusion = (bf16[8,192,256]{2,1,0:T(8,128)(2,1)}, bf16[8,192,256]{2,1,0:T(8,128)(2,1)}) fusion(bf16[192,8,256]{2,1,0:T(8,128)(2,1)} %param.5, bf16[192,8,256]{2,1,0:T(8,128)(2,1)} %param.3), kind=kLoop, calls=%fused_computation | loop fusion | bytes 3145728 | tf_op jit(solution)/shard_map/transpose | solution.py:460
  3.5 128.5 %shard_map.58 = (bf16[8,192,256]{2,1,0:T(8,128)(2,1)}, bf16[8,192,256]{2,1,0:T(8,128)(2,1)}, bf16[10368,128]{1,0:T(8,128)(2,1)}) custom-call(bf16[8,192,256]{2,1,0:T(8,128)(2,1)} %get-tuple-element.13.x_ref, bf16[8,192,256]{2,1,0:T(8,128)(2,1)} %get-tuple-element.12.ct_ref, bf16[9,192,768]{2,1,0:T(8,128)(2,1)} %bitcast.10), custom_call_target="tpu_custom_call" | custom-call | tf_op jit(solution)/shard_map/pallas_call | solution.py:467
  132.0 2.4 %copy.8 = bf16[192,8,256]{2,1,0:T(8,128)(2,1)} copy(bf16[192,8,256]{2,0,1:T(8,128)(2,1)} %bitcast.13) | data formatting | bytes 1572864
  134.4 2.4 %copy.9 = bf16[192,8,256]{2,1,0:T(8,128)(2,1)} copy(bf16[192,8,256]{2,0,1:T(8,128)(2,1)} %bitcast.12) | data formatting | bytes 1572864
  136.9 6.8 %shard_map.59 = f32[1728,768]{1,0:T(8,128)} custom-call(bf16[6,1728,128]{2,1,0:T(8,128)(2,1)} %bitcast.11), custom_call_target="tpu_custom_call" | custom-call | tf_op jit(solution)/shard_map/pallas_call | solution.py:502

commit v4 on v3

--- a/solution.py
+++ b/solution.py
@@ -163,8 +163,13 @@
                 def _():
                     gather_copy(way, step, p, block).wait_recv()
 
-            if step < n - 2:
-                start_gather(step + 1, p)
+                if step < n - 2:
+                    onward, more = sends(way, step + 1)
+
+                    @pl.when(more)
+                    def _():
+                        gather_copy(way, step + 1, p, onward).start()
+
         for way in range(2):
             block, valid = receives(way, step)
 
@@ -501,9 +506,9 @@
     wg = wg[:rows].reshape(lanes, 9 * O, 128)
     weight_grad = pl.pallas_call(
         widen_kernel,
-        grid=(9,),
-        in_specs=[pl.BlockSpec((lanes, O, 128), lambda k: (0, k, 0))],
-        out_specs=pl.BlockSpec((O, n * Cb), lambda k: (k, 0)),
+        grid=(3,),
+        in_specs=[pl.BlockSpec((lanes, T, 128), lambda k: (0, k, 0))],
+        out_specs=pl.BlockSpec((T, n * Cb), lambda k: (k, 0)),
         out_shape=jax.ShapeDtypeStruct((9 * O, n * Cb), F32),
     )(wg)
     return (

time: 146 us -> 143 us (0.979)
  Pallas kernels: 135 us -> 133 us
    pallas_call x1, Pallas kernels: 6.79 us -> 4.49 us  [on_device(): pl.pallas_call(widen_kernel, grid=(3,), in_specs=[pl.BlockSpec((lanes, T,...]
where the time goes in v4:
time: 143 us; the launch traced here: 141 us
  Pallas kernels  133 us (93%)
  local copies, waits for them, and re-layouts  7.75 us (5%)
    pallas_call x1, Pallas kernels, on_device(): pl.pallas_call(functools.partial(kernel, n, S), out_shape=(jax.ShapeDtype...  128 us
    unnamed x2, local copies, waits for them, and re-layouts  4.9 us
    pallas_call x1, Pallas kernels, on_device(): pl.pallas_call(widen_kernel, grid=(3,), in_specs=[pl.BlockSpec((lanes, T,...  4.49 us

profile of v4, /device:TPU:0, one launch (start us, length us, event | category | flops | bytes accessed | tf_op | source)
XLA Modules:
  0.0 141.4 jit_solution(7933435081486634107)
XLA Ops:
  0.6 2.9 %copy_bitcast_fusion = (bf16[8,192,256]{2,1,0:T(8,128)(2,1)}, bf16[8,192,256]{2,1,0:T(8,128)(2,1)}) fusion(bf16[192,8,256]{2,1,0:T(8,128)(2,1)} %param.5, bf16[192,8,256]{2,1,0:T(8,128)(2,1)} %param.3), kind=kLoop, calls=%fused_computation | loop fusion | bytes 3145728 | tf_op jit(solution)/shard_map/transpose | solution.py:465
  3.5 128.5 %shard_map.58 = (bf16[8,192,256]{2,1,0:T(8,128)(2,1)}, bf16[8,192,256]{2,1,0:T(8,128)(2,1)}, bf16[10368,128]{1,0:T(8,128)(2,1)}) custom-call(bf16[8,192,256]{2,1,0:T(8,128)(2,1)} %get-tuple-element.13.x_ref, bf16[8,192,256]{2,1,0:T(8,128)(2,1)} %get-tuple-element.12.ct_ref, bf16[9,192,768]{2,1,0:T(8,128)(2,1)} %bitcast.10), custom_call_target="tpu_custom_call" | custom-call | tf_op jit(solution)/shard_map/pallas_call | solution.py:472
  132.0 2.4 %copy.8 = bf16[192,8,256]{2,1,0:T(8,128)(2,1)} copy(bf16[192,8,256]{2,0,1:T(8,128)(2,1)} %bitcast.13) | data formatting | bytes 1572864
  134.4 2.4 %copy.9 = bf16[192,8,256]{2,1,0:T(8,128)(2,1)} copy(bf16[192,8,256]{2,0,1:T(8,128)(2,1)} %bitcast.12) | data formatting | bytes 1572864
  136.9 4.5 %shard_map.59 = f32[1728,768]{1,0:T(8,128)} custom-call(bf16[6,1728,128]{2,1,0:T(8,128)(2,1)} %bitcast.11), custom_call_target="tpu_custom_call" | custom-call | tf_op jit(solution)/shard_map/pallas_call | solution.py:507
